TPU v7x, 128 devices: a whole 4x4x4 slice. The times are simulated.
128 devices in a mesh: table: 8 (over y, core), seq: 16 (over z, x).
Axes of the slice: x: 4, y: 4, z: 4, core: 2. Of those that a mesh axis runs over, the one named last changes fastest.
Arguments:
- item_ids: int32 [8, 4096], P('table', 'seq'), may hold values from 0 to 524287, as said below
- history_len: int32 [8], P('table'), may hold values from 1024 to 4096, as said below
- row_place: int32 [524288], replicated, may hold values from 0 to 524287, as said below
- item_table: bfloat16 [524288, 512], P(('table', 'seq')), may hold values from -6 to 6
- input_proj: bfloat16 [512, 2048], replicated, may hold values from -0.25 to 0.25
- output_proj: bfloat16 [512, 512], replicated, may hold values from -0.25 to 0.25
- out_cotangent: bfloat16 [8, 4096, 512], P('table', 'seq'), may hold values from -18 to 18
Outputs:
- layer_out: bfloat16 [8, 4096, 512], P('table', 'seq')
- table_grad: bfloat16 [524288, 512], P(('table', 'seq'))
Inputs may be any that keep to these rules, and one draw needn't show every extreme that they name: `item_ids`: within the 256 positions of one device, at most 6 items are stored in any one owner's block of 4096 table rows (rows o * 4096 to (o + 1) * 4096 - 1); one owner's block receives exactly 6 from the positions of every device. `row_place`: A permutation: every table row holds exactly one item. `history_len`: at least one history fills all 4096 positions.
All inputs are finite; a program needn't handle non-finite values.
Results may differ from a plain program's by a relative error of at most 0.006.
Values may be sent and summed in bfloat16 or wider, within the bound.
A program may use at most 128 MiB of HBM per device.

v0:
```python
import math
import jax
import jax.numpy as jnp
from jax import lax
from jax.sharding import PartitionSpec as P

HEADS = 8
eps_norm = 1e-05
block_limit = 512


def dsilu(inputs):
    sigmoid_part = jax.nn.sigmoid(inputs)
    return sigmoid_part * (1.0 + inputs * (1.0 - sigmoid_part))


def normalize(inputs):
    centred = inputs - jnp.mean(inputs, axis=-1, keepdims=True)
    spread = jnp.sqrt(jnp.mean(centred * centred, axis=-1, keepdims=True) + eps_norm)
    return (centred / spread, spread)


def norm_back(gradient, normed, spread):
    mean_grad = jnp.mean(gradient, axis=-1, keepdims=True)
    mean_prod = jnp.mean(gradient * normed, axis=-1, keepdims=True)
    return (gradient - mean_grad - normed * mean_prod) / spread


def heads_view(matrix):
    return matrix.reshape(matrix.shape[0], HEADS, matrix.shape[1] // HEADS)


def tile_mask(query_pos, key_pos, length_user):
    return (key_pos[None, :] <= query_pos[:, None]) & (query_pos[:, None] < length_user)


def tile_forward(queries, keys_blk, values_blk, allowed, score_scale):
    scores = (
        jnp.einsum(
            "lhe,nhe->hln",
            heads_view(queries),
            heads_view(keys_blk),
            preferred_element_type=jnp.float32,
        )
        * score_scale
    )
    weights = jnp.where(allowed[None], jax.nn.silu(scores), 0.0).astype(jnp.bfloat16)
    result = jnp.einsum(
        "hln,nhe->lhe", weights, heads_view(values_blk), preferred_element_type=jnp.float32
    )
    return result.reshape(queries.shape[0], -1)


def tile_query_grad(queries, grad_rows, keys_blk, values_blk, allowed, score_scale):
    scores = (
        jnp.einsum(
            "lhe,nhe->hln",
            heads_view(queries),
            heads_view(keys_blk),
            preferred_element_type=jnp.float32,
        )
        * score_scale
    )
    weight_grad = jnp.einsum(
        "lhe,nhe->hln",
        heads_view(grad_rows),
        heads_view(values_blk),
        preferred_element_type=jnp.float32,
    )
    score_grad = jnp.where(allowed[None], weight_grad * dsilu(scores), 0.0).astype(jnp.bfloat16)
    result = jnp.einsum(
        "hln,nhe->lhe", score_grad, heads_view(keys_blk), preferred_element_type=jnp.float32
    )
    return result.reshape(queries.shape[0], -1) * score_scale


def tile_key_grad(query_piece, grad_piece, keys_mine, values_mine, allowed, score_scale):
    scores = (
        jnp.einsum(
            "lhe,nhe->hln",
            heads_view(query_piece),
            heads_view(keys_mine),
            preferred_element_type=jnp.float32,
        )
        * score_scale
    )
    weights = jnp.where(allowed[None], jax.nn.silu(scores), 0.0).astype(jnp.bfloat16)
    weight_grad = jnp.einsum(
        "lhe,nhe->hln",
        heads_view(grad_piece),
        heads_view(values_mine),
        preferred_element_type=jnp.float32,
    )
    score_grad = jnp.where(allowed[None], weight_grad * dsilu(scores), 0.0).astype(jnp.bfloat16)
    value_part = jnp.einsum(
        "hln,lhe->nhe", weights, heads_view(grad_piece), preferred_element_type=jnp.float32
    )
    key_part = jnp.einsum(
        "hln,lhe->nhe", score_grad, heads_view(query_piece), preferred_element_type=jnp.float32
    )
    key_count = keys_mine.shape[0]
    return (key_part.reshape(key_count, -1) * score_scale, value_part.reshape(key_count, -1))


def over_blocks(tile_fn, running, pieces):
    rows_in = pieces[0].shape[0]
    block_rows = math.gcd(rows_in, block_limit)
    block_count = rows_in // block_rows
    stacked = tuple(
        (member.reshape((block_count, block_rows) + member.shape[1:]) for member in pieces)
    )
    offsets = jnp.arange(block_count, dtype=jnp.int32) * block_rows

    def step_block(carried, scan_item):
        offset, blocks_now = scan_item
        return (tile_fn(carried, blocks_now, offset), None)

    result, unused = lax.scan(step_block, running, (offsets, stacked))
    return result


def local(item_ids, history_len, row_place, item_table, input_proj, output_proj, out_cotangent):
    ids_local = item_ids[0]
    length_user = history_len[0]
    seq_len = ids_local.shape[0]
    rows_dev = item_table.shape[0]
    model_width = item_table.shape[1]
    score_scale = (model_width // HEADS) ** (-0.5)
    table_count = lax.axis_size("table")
    seq_count = lax.axis_size("seq")
    owners = table_count * seq_count
    capacity = 3 * seq_len // owners
    query_first = lax.axis_index("seq") * seq_len
    positions = query_first + jnp.arange(seq_len, dtype=jnp.int32)
    live_rows = (positions < length_user).astype(jnp.float32)[:, None]
    stored = row_place[ids_local]
    owner_of = stored // rows_dev
    local_row = stored % rows_dev
    owner_hits = (owner_of[:, None] == jnp.arange(owners, dtype=jnp.int32)[None, :]).astype(
        jnp.int32
    )
    slot_rank = jnp.sum((jnp.cumsum(owner_hits, axis=0) - owner_hits) * owner_hits, axis=1)
    slot_of = owner_of * capacity + slot_rank
    requests = jnp.full((owners * capacity,), -1, jnp.int32).at[slot_of].set(local_row)
    wanted = lax.all_to_all(
        requests.reshape(owners, capacity),
        ("table", "seq"),
        split_axis=0,
        concat_axis=0,
        tiled=True,
    )
    safe_rows = jnp.maximum(wanted, 0)
    returned = lax.all_to_all(
        jnp.where((wanted >= 0)[..., None], item_table[safe_rows], 0.0),
        ("table", "seq"),
        split_axis=0,
        concat_axis=0,
        tiled=True,
    )
    answered = returned
    asked_rows = wanted
    answered = answered.reshape(owners * capacity, model_width)
    asked_rows = asked_rows.reshape(owners * capacity)
    embedded = answered[slot_of]
    normed_exact, input_spread = normalize(embedded.astype(jnp.float32))
    normed = normed_exact.astype(jnp.bfloat16)
    pre_act = jnp.dot(normed, input_proj, preferred_element_type=jnp.float32)
    activated = jax.nn.silu(pre_act)
    gate_u = activated[:, :model_width]
    values_loc = activated[:, model_width : 2 * model_width].astype(jnp.bfloat16)
    queries_loc = activated[:, 2 * model_width : 3 * model_width].astype(jnp.bfloat16)
    keys_loc = activated[:, 3 * model_width :].astype(jnp.bfloat16)
    zero_rows = jnp.zeros((seq_len, model_width), jnp.float32)

    def forward_tile(running, pieces_blk, key_start):
        keys_blk, values_blk = pieces_blk
        key_pos = key_start + jnp.arange(keys_blk.shape[0], dtype=jnp.int32)
        allowed = tile_mask(positions, key_pos, length_user)
        return running + tile_forward(queries_loc, keys_blk, values_blk, allowed, score_scale)

    attention = over_blocks(
        forward_tile,
        zero_rows,
        (
            lax.all_gather(keys_loc, "seq", axis=0, tiled=True),
            lax.all_gather(values_loc, "seq", axis=0, tiled=True),
        ),
    )
    attn_normed, attn_spread = normalize(attention)
    mixed = (attn_normed * gate_u).astype(jnp.bfloat16)
    branch = jnp.dot(mixed, output_proj, preferred_element_type=jnp.float32)
    layer_out = (live_rows * (embedded.astype(jnp.float32) + branch)).astype(jnp.bfloat16)
    cot_masked = jnp.where(live_rows > 0.0, out_cotangent[0], 0.0)
    mixed_grad = jnp.einsum(
        "ld,ed->le", cot_masked, output_proj, preferred_element_type=jnp.float32
    )
    attention_grad = norm_back(mixed_grad * gate_u, attn_normed, attn_spread).astype(jnp.bfloat16)

    def query_tile(running, pieces_blk, key_start):
        keys_blk, values_blk = pieces_blk
        key_pos = key_start + jnp.arange(keys_blk.shape[0], dtype=jnp.int32)
        allowed = tile_mask(positions, key_pos, length_user)
        return running + tile_query_grad(
            queries_loc, attention_grad, keys_blk, values_blk, allowed, score_scale
        )

    query_grad = over_blocks(
        query_tile,
        zero_rows,
        (
            lax.all_gather(keys_loc, "seq", axis=0, tiled=True),
            lax.all_gather(values_loc, "seq", axis=0, tiled=True),
        ),
    )

    def key_tile(running, pieces_blk, query_start):
        query_piece, grad_piece = pieces_blk
        rows_in = query_piece.shape[0]
        query_pos = query_start + jnp.arange(rows_in, dtype=jnp.int32)
        allowed = tile_mask(query_pos, positions, length_user)
        key_part, value_part = tile_key_grad(
            query_piece, grad_piece, keys_loc, values_loc, allowed, score_scale
        )
        return (running[0] + key_part, running[1] + value_part)

    key_grad, value_grad = over_blocks(
        key_tile,
        (zero_rows, zero_rows),
        (
            lax.all_gather(queries_loc, "seq", axis=0, tiled=True),
            lax.all_gather(attention_grad, "seq", axis=0, tiled=True),
        ),
    )
    activated_grad = jnp.concatenate(
        [mixed_grad * attn_normed, value_grad, query_grad, key_grad], axis=1
    )
    pre_grad = (activated_grad * dsilu(pre_act)).astype(jnp.bfloat16)
    norm_grad = jnp.einsum("lf,df->ld", pre_grad, input_proj, preferred_element_type=jnp.float32)
    embed_grad = cot_masked.astype(jnp.float32) + norm_back(norm_grad, normed_exact, input_spread)
    outgoing = jnp.zeros((owners * capacity, model_width), jnp.float32).at[slot_of].set(embed_grad)
    arrived = lax.all_to_all(
        outgoing.reshape(owners, capacity, model_width).astype(jnp.bfloat16),
        ("table", "seq"),
        split_axis=0,
        concat_axis=0,
        tiled=True,
    ).astype(jnp.float32)
    arrived = arrived.reshape(owners * capacity, model_width)
    arrived = jnp.where((asked_rows >= 0)[:, None], arrived, 0.0)
    table_sum = (
        jnp.zeros((rows_dev, model_width), jnp.float32).at[jnp.maximum(asked_rows, 0)].add(arrived)
    )
    return (layer_out[None], table_sum.astype(jnp.bfloat16))


def solution(mesh):
    placed = (
        P("table", "seq"),
        P("table"),
        P(),
        P(("table", "seq"), None),
        P(),
        P(),
        P("table", "seq", None),
    )
    return jax.shard_map(
        local,
        mesh=mesh,
        in_specs=placed,
        out_specs=(P("table", "seq", None), P(("table", "seq"), None)),
        check_vma=False,
    )
```

profile of v0, /device:TPU:1, one launch (start us, length us, event | category | flops | bytes accessed | tf_op | source)
XLA Modules:
  0.0 639.1 jit_solution(17129103487321654110)
XLA Ops:
  13.7 21.1 %all_to_all.19 = s32[128,1,6]{2,1,0:T(1,128)S(1)} all-to-all(s32[128,1,6]{2,1,0:T(1,128)S(1)} %bitcast.235), channel_id=1, replica_groups=mesh['table'=8,'seq'=16] {'table','seq'}, dimensions={0} | all-to-all | bytes 6144 | tf_op jit(solution)/shard_map/all_to_all | solution.py:145
  36.3 5.4 gather_fusion.1
  45.5 5.2 all-to-all-start.1
  50.8 19.0 %all-to-all-done.1 = bf16[128,6,512]{2,1,0:T(8,128)(2,1)} async-done(((bf16[128,6,512]{2,1,0:T(8,128)(2,1)}), bf16[128,6,512]{2,1,0:T(8,128)(2,1)}, u32[]{:S(2)}, u32[]{:S(2)}) %all-to-all-start.1) | async-done | bytes 786464 | tf_op jit(solution)/shard_map/all_to_all | solution.py:153
  83.4 40.5 %all-gather.5.cloned.1.call-done = bf16[4096,512]{1,0:T(8,128)(2,1)} async-done(((bf16[256,512]{1,0:T(8,128)(2,1)}), bf16[4096,512]{1,0:T(8,128)(2,1)}) %all-gather.5.cloned.1.call-update) | async-done | bytes 4194320 | tf_op jit(solution)/shard_map/all_gather | solution.py:186
  124.0 6.4 %copy.71 = bf16[8,512,512]{1,2,0:T(8,128)(2,1)} copy(bf16[8,512,512]{2,1,0:T(8,128)(2,1)} %bitcast.227) | data formatting | bytes 8388608
  130.4 47.0 %all-gather.7.cloned.1.call-done = bf16[4096,512]{1,0:T(8,128)(2,1)} async-done(((bf16[256,512]{1,0:T(8,128)(2,1)}), bf16[4096,512]{1,0:T(8,128)(2,1)}) %all-gather.7.cloned.1.call-update) | async-done | bytes 4194320 | tf_op jit(solution)/shard_map/all_gather | solution.py:185
  177.4 6.5 %copy.72 = bf16[8,512,512]{1,2,0:T(8,128)(2,1)} copy(bf16[8,512,512]{2,1,0:T(8,128)(2,1)} %bitcast.228) | data formatting | bytes 8388608
  183.8 79.6 %while.35 = (s32[]{:T(128)}, f32[256,512]{0,1:T(8,128)S(1)}, bf16[8,512,512]{1,2,0:T(8,128)(2,1)}, s32[8]{0:T(128)}, s32[]{:T(128)}, /*index=5*/bf16[8,512,512]{...) while((s32[]{:T(128)}, f32[256,512]{0,1:T(8,128)S(1)}, ...), condition=%wide.region_7.8_spmd.clone, body=%wide.region_6.7_spmd.clone.sunk | while | flops 276301056 | bytes 5773967 | solution.py:118
  270.8 120.8 %while.37 = (s32[]{:T(128)}, f32[256,512]{0,1:T(8,128)S(1)}, bf16[8,512,512]{1,2,0:T(8,128)(2,1)}, s32[8]{0:T(128)}, s32[]{:T(128)}, /*index=5*/bf16[8,512,512]{...) while((s32[]{:T(128)}, f32[256,512]{0,1:T(8,128)S(1)}, ...), condition=%wide.region_15.16_spmd.clone, body=%wide.region_14.15_spmd.clone.sunk | while | flops 414844160 | bytes 14949015 | solution.py:118
  279.2 5.6 fusion.144
  294.4 5.5 fusion.144
  309.5 5.6 fusion.144
  324.7 5.5 fusion.144
  339.8 5.4 fusion.144
  354.8 5.5 fusion.144
  369.9 5.4 fusion.144
  384.9 5.4 fusion.144
  392.6 177.3 %while.36 = (s32[]{:T(128)}, f32[256,512]{0,1:T(8,128)}, f32[256,512]{0,1:T(8,128)}, bf16[8,512,512]{2,1,0:T(8,128)(2,1)}, s32[8]{0:T(128)}, /*index=5*/s32[]{:T...) while((s32[]{:T(128)}, f32[256,512]{0,1:T(8,128)}, ...), condition=%wide.region_13.14_spmd.clone, body=%wide.region_12.13_spmd.clone.sunk | while | flops 556664576 | bytes 32382224 | solution.py:118
  402.4 5.5 fusion.137
  424.5 5.5 fusion.137
  430.0 4.6 fusion.136
  446.7 5.5 fusion.137
  468.8 5.5 fusion.137
  491.0 5.5 fusion.137
  513.1 5.5 fusion.137
  535.2 5.5 fusion.137
  557.4 5.5 fusion.137
  584.4 8.1 %all-to-all-start.2 = ((bf16[128,6,512]{2,1,0:T(8,128)(2,1)}), bf16[128,6,512]{2,1,0:T(8,128)(2,1)}, u32[]{:S(2)}, u32[]{:S(2)}) async-start(bf16[128,6,512]{2,1,0:T(8,128)(2,1)} %convert_element_type.79), calls=%async_computation.2 | async-start | bytes 2097152 | tf_op jit(solution)/shard_map/all_to_all | solution.py:241
  595.0 16.4 %all-to-all-done.2 = bf16[128,6,512]{2,1,0:T(8,128)(2,1)} async-done(((bf16[128,6,512]{2,1,0:T(8,128)(2,1)}), bf16[128,6,512]{2,1,0:T(8,128)(2,1)}, u32[]{:S(2)}, u32[]{:S(2)}) %all-to-all-start.2) | async-done | bytes 786464 | tf_op jit(solution)/shard_map/all_to_all | solution.py:241
  613.8 12.8 %scatter_custom_fusion.2 = f32[4096,512]{1,0:T(8,128)} fusion(s32[768]{0:T(1024)} %copy-done.12, f32[]{:T(128)} %constant.119.clone.1, f32[768,512]{1,0:T(8,128)} %reshape.445, pred[768]{0:T(1024)(128)(4,1)S(1)} %ge.20), kind=kCustom, calls=%fused_computation.69 | custom fusion | flops 786432 | bytes 9963264 | tf_op jit(solution)/shard_map/scatter-add | solution.py:251
  626.6 5.9 convert_element_type.80
  (399 shorter events, 336.2 us)
Async XLA Ops:
  7.2 65.6 %copy-start = (bf16[512,2048]{1,0:T(8,128)(2,1)S(1)}, bf16[512,2048]{1,0:T(8,128)(2,1)}, u32[]{:S(2)}) copy-start(bf16[512,2048]{1,0:T(8,128)(2,1)} %param.17) | copy-start | bytes 6291460
  12.1 38.7 %copy-start.17 = (s32[256,1]{0,1:T(1,128)}, s32[256,1]{0,1:T(1,128)S(1)}, u32[]{:S(2)}) copy-start(s32[256,1]{0,1:T(1,128)S(1)} %compare_select_fusion) | copy-start | bytes 3076
  45.5 24.3 %all-to-all-start.1 = ((bf16[128,6,512]{2,1,0:T(8,128)(2,1)}), bf16[128,6,512]{2,1,0:T(8,128)(2,1)}, u32[]{:S(2)}, u32[]{:S(2)}) async-start(bf16[128,6,512]{2,1,0:T(8,128)(2,1)} %broadcast_select_fusion), calls=%async_computation.1 | async-start | bytes 2097152 | tf_op jit(solution)/shard_map/all_to_all | solution.py:153
  50.8 73.2 %all-gather.5.cloned.1.call-start = ((), (), s32[]{:S(2)}) async-start(), calls=%async_computation.3 | async-start | bytes 4456448 | tf_op jit(solution)/shard_map/all_gather | solution.py:186
  76.5 100.9 %all-gather.7.cloned.1.call-start = ((), (), s32[]{:S(2)}) async-start(), calls=%async_computation.4 | async-start | bytes 4456448 | tf_op jit(solution)/shard_map/all_gather | solution.py:185
  77.2 315.4 %all-gather.9.cloned.1.call-start = ((), (), s32[]{:S(2)}) async-start(), calls=%async_computation.5 | async-start | bytes 4456448 | tf_op jit(solution)/shard_map/all_gather | solution.py:230
  78.5 187.4 %copy-start.18 = (pred[256]{0:T(512)(128)(4,1)}, pred[256]{0:T(512)(128)(4,1)S(1)}, u32[]{:S(2)}) copy-start(pred[256]{0:T(512)(128)(4,1)S(1)} %broadcast_compare_fusion.4) | copy-start | bytes 772
  83.2 309.4 %all-gather.11.cloned.1.call-start = ((), (), s32[]{:S(2)}) async-start(), calls=%async_computation.6 | async-start | bytes 4456448 | tf_op jit(solution)/shard_map/all_gather | solution.py:231
  392.6 179.8 %copy-start.14 = (f32[256]{0:T(256)S(1)}, f32[256]{0:T(256)}, u32[]{:S(2)}) copy-start(f32[256]{0:T(256)} %copy-done.13) | copy-start | bytes 3076
  392.6 179.9 %copy-start.16 = (f32[256]{0:T(256)S(1)}, f32[256]{0:T(256)}, u32[]{:S(2)}) copy-start(f32[256]{0:T(256)} %copy-done.15) | copy-start | bytes 3076
  407.9 4.6 copy-start.1
  407.9 4.6 copy-start.3
  430.0 4.6 copy-start.1
  430.0 4.6 copy-start.3
  452.1 4.6 copy-start.1
  452.1 4.6 copy-start.3
  474.3 4.6 copy-start.1
  474.3 4.6 copy-start.3
  496.4 4.6 copy-start.1
  496.4 4.6 copy-start.3
  518.6 4.6 copy-start.1
  518.6 4.6 copy-start.3
  540.7 4.6 copy-start.1
  540.7 4.6 copy-start.3
  562.8 4.6 copy-start.1
  562.8 4.6 copy-start.3
  572.5 3.8 copy-start.8
  572.5 3.8 copy-start.19
  576.3 16.2 %copy-start.11 = (s32[128,1,6]{0,2,1:T(8,128)S(1)}, s32[128,1,6]{0,2,1:T(8,128)}, u32[]{:S(2)}) copy-start(s32[128,1,6]{0,2,1:T(8,128)} %copy-done.10) | copy-start | bytes 9220
  576.3 16.5 %copy-start.6 = (f32[256,512]{1,0:T(8,128)S(1)}, f32[256,512]{1,0:T(8,128)}, u32[]{:S(2)}) copy-start(f32[256,512]{1,0:T(8,128)} %copy.74) | copy-start | bytes 1572868
  579.8 13.0 %copy-start.20 = (bf16[512,512]{1,0:T(8,128)(2,1)S(1)}, bf16[512,512]{1,0:T(8,128)(2,1)}, u32[]{:S(2)}) copy-start(bf16[512,512]{1,0:T(8,128)(2,1)} %param.18) | copy-start | bytes 1572868
  584.4 27.0 %all-to-all-start.2 = ((bf16[128,6,512]{2,1,0:T(8,128)(2,1)}), bf16[128,6,512]{2,1,0:T(8,128)(2,1)}, u32[]{:S(2)}, u32[]{:S(2)}) async-start(bf16[128,6,512]{2,1,0:T(8,128)(2,1)} %convert_element_type.79), calls=%async_computation.2 | async-start | bytes 2097152 | tf_op jit(solution)/shard_map/all_to_all | solution.py:241
  (23 other events, 28.9 us)
Sparse Core Ops, SparseCore 0:
  76.6 47.3 all-gather.4
  126.1 51.2 all-gather.6
  179.5 51.2 all-gather.8
  270.9 51.2 all-gather.10
where the time goes:
time: 644 us; the launch traced here: 639 us
  matrix products  216 us (34%)
  local copies, waits for them, and re-layouts  143 us (22%)
  waiting for transfers between devices  124 us (19%)
  other arithmetic  104 us (16%)
  blocking collectives  21.1 us (3%)
  between operations  14.9 us (2%)
  starting transfers between devices  13.7 us (2%)
    dynamic_slice x72, local copies, waits for them, and re-layouts, over_blocks(): result, unused = lax.scan(step_block, running, (offsets, stacked))  90.7 us
    all_gather x1, waiting for transfers between devices, local(): lax.all_gather(keys_loc, 'seq', axis=0, tiled=True)  47 us
    dot_general x8, matrix products, tile_query_grad(): jnp.einsum('hln,nhe->lhe', score_grad, heads_view(keys_blk), preferred_el...  43.9 us
    dot_general x8, matrix products, tile_key_grad(): jnp.einsum('hln,lhe->nhe', score_grad, heads_view(query_piece), preferred...  43.6 us
    all_gather x1, waiting for transfers between devices, local(): lax.all_gather(values_loc, 'seq', axis=0, tiled=True)  40.5 us
    dot_general x8, matrix products, tile_key_grad(): jnp.einsum('hln,lhe->nhe', weights, heads_view(grad_piece), preferred_ele...  36.6 us
    dot_general x8, matrix products, tile_forward(): jnp.einsum('hln,nhe->lhe', weights, heads_view(values_blk), preferred_ele...  30.6 us
    dot_general x8, matrix products, tile_query_grad(): jnp.einsum('lhe,nhe->hln', heads_view(queries), heads_view(keys_blk), pre...  29.1 us
  transfers between devices with their start and end apart: 6, of which 4 were waited for; matrix products, arithmetic and copies ran while one was open for 36% of the time, Pallas kernels for 0%

commit v1 on v0

--- a/solution.py
+++ b/solution.py
@@ -7,6 +7,11 @@
 HEADS = 8
 eps_norm = 1e-05
 block_limit = 512
+
+
+def all_by_exchange(shard, axis, along):
+    stack = jnp.stack([shard] * lax.axis_size(axis))
+    return jnp.concatenate(lax.all_to_all(stack, axis, 0, 0), axis=along)
 
 
 def dsilu(inputs):
@@ -182,7 +187,7 @@
         forward_tile,
         zero_rows,
         (
-            lax.all_gather(keys_loc, "seq", axis=0, tiled=True),
+            all_by_exchange(keys_loc, "seq", 0),
             lax.all_gather(values_loc, "seq", axis=0, tiled=True),
         ),
     )

time: 644 us -> 651 us (1.011)
  local copies, waits for them, and re-layouts: 143 us -> 169 us
  other arithmetic: 104 us -> 95.4 us
  waiting for transfers between devices: 124 us -> 117 us
    all_gather x1, waiting for transfers between devices: 47 us -> 0.02 us  [local(): lax.all_gather(keys_loc, 'seq', axis=0, tiled=True)]
    all_gather x1, waiting for transfers between devices: 40.5 us -> 80.5 us  [local(): lax.all_gather(values_loc, 'seq', axis=0, tiled=True)]
    dynamic_slice x72 -> x104, local copies, waits for them, and re-layouts: 90.7 us -> 115 us  [over_blocks(): result, unused = lax.scan(step_block, running, (offsets, stacked))]
    unnamed x41 -> x46, local copies, waits for them, and re-layouts: 19.7 us -> 10.4 us
    add x8, other arithmetic: 9.44 us -> 0.98 us  [forward_tile(): running + tile_forward(queries_loc, keys_blk, values_blk, allowed, score_...]
    while x64 -> x96, local copies, waits for them, and re-layouts: 7.91 us -> 14.7 us
  transfers between devices with their start and end apart: 6 -> 7, of which waited for: 4 -> 3; matrix products, arithmetic and copies ran while one was open for 36% -> 36% of each run, Pallas kernels for 0% -> 0%
where the time goes in v1:
time: 651 us; the launch traced here: 645 us
  matrix products  210 us (32%)
  local copies, waits for them, and re-layouts  169 us (26%)
  waiting for transfers between devices  117 us (18%)
  other arithmetic  95.4 us (15%)
  blocking collectives  21.1 us (3%)
  starting transfers between devices  16.3 us (3%)
  between operations  14.9 us (2%)
    dynamic_slice x104, local copies, waits for them, and re-layouts, over_blocks(): result, unused = lax.scan(step_block, running, (offsets, stacked))  115 us
    all_gather x1, waiting for transfers between devices, local(): lax.all_gather(values_loc, 'seq', axis=0, tiled=True)  80.5 us
    dot_general x8, matrix products, tile_query_grad(): jnp.einsum('hln,nhe->lhe', score_grad, heads_view(keys_blk), preferred_el...  44.6 us
    dot_general x8, matrix products, tile_key_grad(): jnp.einsum('hln,lhe->nhe', score_grad, heads_view(query_piece), preferred...  43.7 us
    dot_general x8, matrix products, tile_key_grad(): jnp.einsum('hln,lhe->nhe', weights, heads_view(grad_piece), preferred_ele...  36.2 us
    dot_general x8, matrix products, tile_query_grad(): jnp.einsum('lhe,nhe->hln', heads_view(queries), heads_view(keys_blk), pre...  29 us
    dot_general x8, matrix products, tile_forward(): jnp.einsum('hln,nhe->lhe', weights, heads_view(values_blk), preferred_ele...  24.2 us
    dot_general x8, matrix products, tile_key_grad(): jnp.einsum('lhe,nhe->hln', heads_view(query_piece), heads_view(keys_mine)...  22.2 us
  transfers between devices with their start and end apart: 7, of which 3 were waited for; matrix products, arithmetic and copies ran while one was open for 36% of the time, Pallas kernels for 0%

profile of v1, /device:TPU:1, one launch (start us, length us, event | category | flops | bytes accessed | tf_op | source)
XLA Modules:
  0.0 645.4 jit_solution(8881724493695512591)
XLA Ops:
  13.7 21.1 %all_to_all.24 = s32[128,1,6]{2,1,0:T(1,128)S(1)} all-to-all(s32[128,1,6]{2,1,0:T(1,128)S(1)} %bitcast.236), channel_id=1, replica_groups=mesh['table'=8,'seq'=16] {'table','seq'}, dimensions={0} | all-to-all | bytes 6144 | tf_op jit(solution)/shard_map/all_to_all | solution.py:150
  36.3 5.4 gather_fusion.1
  45.5 5.2 all-to-all-start.1
  50.8 19.0 %all-to-all-done.1 = bf16[128,6,512]{2,1,0:T(8,128)(2,1)} async-done(((bf16[128,6,512]{2,1,0:T(8,128)(2,1)}), bf16[128,6,512]{2,1,0:T(8,128)(2,1)}, u32[]{:S(2)}, u32[]{:S(2)}) %all-to-all-start.1) | async-done | bytes 786464 | tf_op jit(solution)/shard_map/all_to_all | solution.py:158
  80.5 4.7 all-to-all-start.2
  88.7 80.5 %all-gather.5.cloned.1.call-done = bf16[4096,512]{1,0:T(8,128)(2,1)} async-done(((bf16[256,512]{1,0:T(8,128)(2,1)}), bf16[4096,512]{1,0:T(8,128)(2,1)}) %all-gather.5.cloned.1.call-update) | async-done | bytes 4194320 | tf_op jit(solution)/shard_map/all_gather | solution.py:191
  169.2 6.4 copy.70
  175.6 80.5 %while.35 = (s32[]{:T(128)}, f32[256,512]{0,1:T(8,128)S(1)}, bf16[8,512,512]{1,2,0:T(8,128)(2,1)}, s32[8]{0:T(128)}, s32[]{:T(128)}, /*index=5*/bf16[8,512,512]{...) while((s32[]{:T(128)}, f32[256,512]{0,1:T(8,128)S(1)}, ...), condition=%wide.region_7.8_spmd.clone, body=%wide.region_6.7_spmd.clone.sunk | while | flops 276301056 | bytes 6822547 | solution.py:123
  261.4 136.9 %while.37 = (s32[]{:T(128)}, f32[256,512]{0,1:T(8,128)}, bf16[8,512,512]{2,1,0:T(8,128)(2,1)}, s32[8]{0:T(128)}, s32[]{:T(128)}, /*index=5*/bf16[8,512,512]{1,2,...) while((s32[]{:T(128)}, f32[256,512]{0,1:T(8,128)}, ...), condition=%wide.region_15.16_spmd.clone, body=%wide.region_14.15_spmd.clone.sunk | while | flops 414844160 | bytes 20191956 | solution.py:123
  271.0 5.5 fusion.144
  288.0 5.5 fusion.144
  305.1 5.9 fusion.144
  322.6 5.5 fusion.144
  339.6 5.5 fusion.144
  356.7 5.5 fusion.144
  373.7 5.5 fusion.144
  390.8 5.5 fusion.144
  400.4 178.0 %while.36 = (s32[]{:T(128)}, f32[256,512]{0,1:T(8,128)}, f32[256,512]{0,1:T(8,128)}, bf16[8,512,512]{2,1,0:T(8,128)(2,1)}, s32[8]{0:T(128)}, /*index=5*/s32[]{:T...) while((s32[]{:T(128)}, f32[256,512]{0,1:T(8,128)}, ...), condition=%wide.region_13.14_spmd.clone, body=%wide.region_12.13_spmd.clone.sunk | while | flops 556664576 | bytes 32382224 | solution.py:123
  410.2 5.5 fusion.137
  415.7 4.5 fusion.136
  432.4 5.5 fusion.137
  454.7 5.5 fusion.137
  476.9 5.5 fusion.137
  499.1 5.5 fusion.137
  504.6 4.5 fusion.136
  521.3 5.5 fusion.137
  543.5 5.5 fusion.137
  565.7 5.5 fusion.137
  592.8 6.1 all-to-all-start.3
  601.3 16.5 %all-to-all-done.3 = bf16[128,6,512]{2,1,0:T(8,128)(2,1)} async-done(((bf16[128,6,512]{2,1,0:T(8,128)(2,1)}), bf16[128,6,512]{2,1,0:T(8,128)(2,1)}, u32[]{:S(2)}, u32[]{:S(2)}) %all-to-all-start.3) | async-done | bytes 786464 | tf_op jit(solution)/shard_map/all_to_all | solution.py:246
  620.1 12.8 %scatter_custom_fusion.2 = f32[4096,512]{1,0:T(8,128)} fusion(s32[768]{0:T(1024)} %copy-done.17, f32[]{:T(128)} %constant.119.clone.1, f32[768,512]{1,0:T(8,128)} %reshape.446, pred[768]{0:T(1024)(128)(4,1)S(1)} %ge.20), kind=kCustom, calls=%fused_computation.69 | custom fusion | flops 786432 | bytes 9963264 | tf_op jit(solution)/shard_map/scatter-add | solution.py:256
  632.9 5.9 convert_element_type.80
  (471 shorter events, 347.8 us)
Async XLA Ops:
  7.2 65.6 %copy-start = (bf16[512,2048]{1,0:T(8,128)(2,1)S(1)}, bf16[512,2048]{1,0:T(8,128)(2,1)}, u32[]{:S(2)}) copy-start(bf16[512,2048]{1,0:T(8,128)(2,1)} %param.17) | copy-start | bytes 6291460
  12.1 38.7 %copy-start.22 = (s32[256,1]{0,1:T(1,128)}, s32[256,1]{0,1:T(1,128)S(1)}, u32[]{:S(2)}) copy-start(s32[256,1]{0,1:T(1,128)S(1)} %compare_select_fusion) | copy-start | bytes 3076
  45.5 24.3 %all-to-all-start.1 = ((bf16[128,6,512]{2,1,0:T(8,128)(2,1)}), bf16[128,6,512]{2,1,0:T(8,128)(2,1)}, u32[]{:S(2)}, u32[]{:S(2)}) async-start(bf16[128,6,512]{2,1,0:T(8,128)(2,1)} %broadcast_select_fusion), calls=%async_computation.1 | async-start | bytes 2097152 | tf_op jit(solution)/shard_map/all_to_all | solution.py:158
  50.8 118.4 %all-gather.5.cloned.1.call-start = ((), (), s32[]{:S(2)}) async-start(), calls=%async_computation.4 | async-start | bytes 4456448 | tf_op jit(solution)/shard_map/all_gather | solution.py:191
  76.5 11.1 %copy-start.13 = (bf16[256,512]{1,0:T(8,128)(2,1)}, bf16[256,512]{1,0:T(8,128)(2,1)S(1)}, u32[]{:S(2)}) copy-start(bf16[256,512]{1,0:T(8,128)(2,1)S(1)} %get-tuple-element.419) | copy-start | bytes 786436
  76.5 184.9 %all-gather.11.cloned.1.call-start = ((), (), s32[]{:S(2)}) async-start(), calls=%async_computation.7 | async-start | bytes 4456448 | tf_op jit(solution)/shard_map/all_gather | solution.py:216
  80.5 6.0 copy-start.14
  80.5 6.9 %copy-start.9 = (bf16[256,512]{1,0:T(8,128)(2,1)S(1)}, bf16[256,512]{1,0:T(8,128)(2,1)}, u32[]{:S(2)}) copy-start(bf16[256,512]{1,0:T(8,128)(2,1)} %get-tuple-element.420) | copy-start | bytes 786436
  80.5 95.1 %all-to-all-start.2 = ((bf16[16,256,512]{2,1,0:T(8,128)(2,1)}), bf16[16,256,512]{2,1,0:T(8,128)(2,1)}, u32[]{:S(2)}, u32[]{:S(2)}) async-start(bf16[16,256,512]{2,1,0:T(8,128)(2,1)} %stack.2), calls=%async_computation.2 | async-start | bytes 8388608 | tf_op jit(solution)/shard_map/all_to_all | solution.py:14
  85.2 315.1 %all-gather.7.cloned.1.call-start = ((), (), s32[]{:S(2)}) async-start(), calls=%async_computation.5 | async-start | bytes 4456448 | tf_op jit(solution)/shard_map/all_gather | solution.py:235
  86.5 170.1 %copy-start.23 = (pred[256]{0:T(512)(128)(4,1)}, pred[256]{0:T(512)(128)(4,1)S(1)}, u32[]{:S(2)}) copy-start(pred[256]{0:T(512)(128)(4,1)S(1)} %broadcast_compare_fusion.4) | copy-start | bytes 772
  88.4 311.9 %all-gather.9.cloned.1.call-start = ((), (), s32[]{:S(2)}) async-start(), calls=%async_computation.6 | async-start | bytes 4456448 | tf_op jit(solution)/shard_map/all_gather | solution.py:236
  256.3 5.1 copy-start.7
  271.0 5.5 copy-start.1
  288.0 5.5 copy-start.1
  305.1 5.9 copy-start.1
  322.6 5.5 copy-start.1
  339.6 5.5 copy-start.1
  356.7 5.5 copy-start.1
  373.7 5.5 copy-start.1
  390.8 5.5 copy-start.1
  400.4 180.5 %copy-start.19 = (f32[256]{0:T(256)S(1)}, f32[256]{0:T(256)}, u32[]{:S(2)}) copy-start(f32[256]{0:T(256)} %copy-done.18) | copy-start | bytes 3076
  400.4 180.5 %copy-start.21 = (f32[256]{0:T(256)S(1)}, f32[256]{0:T(256)}, u32[]{:S(2)}) copy-start(f32[256]{0:T(256)} %copy-done.20) | copy-start | bytes 3076
  415.7 4.5 copy-start.5
  460.1 4.5 copy-start.3
  460.1 4.5 copy-start.5
  504.6 4.5 copy-start.5
  549.0 4.5 copy-start.5
  584.7 14.2 %copy-start.16 = (s32[128,1,6]{0,2,1:T(8,128)S(1)}, s32[128,1,6]{0,2,1:T(8,128)}, u32[]{:S(2)}) copy-start(s32[128,1,6]{0,2,1:T(8,128)} %copy-done.15) | copy-start | bytes 9220
  584.7 14.5 %copy-start.8 = (f32[256,512]{1,0:T(8,128)S(1)}, f32[256,512]{1,0:T(8,128)}, u32[]{:S(2)}) copy-start(f32[256,512]{1,0:T(8,128)} %copy-done.7) | copy-start | bytes 1572868
  588.2 11.0 %copy-start.25 = (bf16[512,512]{1,0:T(8,128)(2,1)S(1)}, bf16[512,512]{1,0:T(8,128)(2,1)}, u32[]{:S(2)}) copy-start(bf16[512,512]{1,0:T(8,128)(2,1)} %param.18) | copy-start | bytes 1572868
  592.8 25.0 %all-to-all-start.3 = ((bf16[128,6,512]{2,1,0:T(8,128)(2,1)}), bf16[128,6,512]{2,1,0:T(8,128)(2,1)}, u32[]{:S(2)}, u32[]{:S(2)}) async-start(bf16[128,6,512]{2,1,0:T(8,128)(2,1)} %convert_element_type.79), calls=%async_computation.3 | async-start | bytes 2097152 | tf_op jit(solution)/shard_map/all_to_all | solution.py:246
  (43 other events, 90.1 us)
Sparse Core Ops, SparseCore 0:
  76.6 92.5 all-gather.4
  171.3 48.8 all-gather.10
  222.3 51.2 all-gather.6
  275.6 51.2 all-gather.8
